TPU v7x, 256 devices: a whole 4x4x8 slice. The times are simulated.
256 devices in a mesh: dp: 32 (over z, x_hi, core), worker: 8 (over y, x_lo).
Axes of the slice: x: 4 (x_hi: 2, x_lo: 2; x = x_hi * 2 + x_lo), y: 4, z: 8, core: 2. Of those that a mesh axis runs over, the one named last changes fastest.
Arguments:
- acts: bfloat16 [32768, 4096], P('dp', 'worker'), may hold values from -6 to 6
- cotan: bfloat16 [32768, 4096], P('dp', 'worker'), may hold values from -0.15625 to 0.15625
- block_ids: int32 [64], P('dp'), may hold values from 0 to 7
- basis_in: bfloat16 [8, 512, 512], P('worker'), may hold values from -0.25 to 0.25
- basis_out: bfloat16 [8, 512, 512], replicated, may hold values from -0.25 to 0.25
- act_factor: float32 [8, 512, 512], P('worker'), may hold values from -0.0009375 to 1, as said below
- grad_factor: float32 [8, 512, 512], P('worker'), may hold values from -0.0009375 to 1, as said below
Outputs:
- precond: bfloat16 [4096, 4096], P('dp', 'worker')
- act_new: float32 [8, 512, 512], P('worker')
- grad_new: float32 [8, 512, 512], P('worker')
Inputs may be any that keep to these rules, and one draw needn't show every extreme that they name: `act_factor`: each block is symmetric, and each diagonal entry exceeds the sum of magnitudes of the other entries of its row. `grad_factor`: each block is symmetric, and each diagonal entry exceeds the sum of magnitudes of the other entries of its row.
All inputs are finite; a program needn't handle non-finite values.
Results may differ from a plain program's by a relative error of at most 0.025.
Values may be sent and summed in bfloat16 or wider, within the bound.
A program may use at most 64 MiB of HBM per device.

v0:
```python
import jax
import jax.numpy as jnp
from jax import lax
from jax.sharding import PartitionSpec as P

BLK = 128


DECAY_RATE = 0.75
DAMPING = 0.03


def per_device(acts, cotan, block_ids, basis_in, basis_out, act_factor, grad_factor):
    highest = lax.Precision.HIGHEST
    n_replicas = lax.axis_size("dp")
    pool_rows, width = acts.shape
    local_blocks, block_size, _ = basis_in.shape
    model_width = basis_out.shape[0] * block_size
    samples = block_ids.shape[0] * BLK * n_replicas
    tokens = pool_rows * n_replicas
    act_pick = jnp.take(acts.reshape(pool_rows // BLK, BLK, width), block_ids, axis=0).reshape(
        -1, local_blocks, block_size
    )
    cot_pick = jnp.take(cotan.reshape(pool_rows // BLK, BLK, width), block_ids, axis=0).reshape(
        -1, local_blocks, block_size
    )
    act_term = (
        jnp.einsum("rbi,rbj->bij", act_pick, act_pick, preferred_element_type=jnp.float32) / samples
    )
    cot_term = jnp.einsum(
        "rbi,rbj->bij", cot_pick, cot_pick, preferred_element_type=jnp.float32
    ) * (tokens / samples)
    act_total, cot_total = (
        lax.psum(act_term.astype(jnp.bfloat16), "dp").astype(jnp.float32),
        lax.psum(cot_term.astype(jnp.bfloat16), "dp").astype(jnp.float32),
    )
    act_new = DECAY_RATE * act_factor + (1.0 - DECAY_RATE) * act_total
    grad_new = DECAY_RATE * grad_factor + (1.0 - DECAY_RATE) * cot_total
    basis_act = basis_in.astype(jnp.float32)
    eig_in = jnp.sum(
        basis_act * jnp.einsum("bij,bjk->bik", act_new, basis_act, precision=highest), axis=1
    )
    local_out = lax.dynamic_slice_in_dim(
        basis_out, lax.axis_index("worker") * local_blocks, local_blocks, 0
    ).astype(jnp.float32)
    eig_local = jnp.sum(
        local_out * jnp.einsum("bij,bjk->bik", grad_new, local_out, precision=highest), axis=1
    )
    eig_out = lax.all_gather(eig_local, "worker", axis=0, tiled=True)
    partial_grad = jnp.einsum(
        "pk,pw->kw",
        lax.all_gather(cotan, "worker", axis=1, tiled=True),
        acts,
        preferred_element_type=jnp.float32,
    )
    rows_dev = model_width // n_replicas
    my_start = lax.axis_index("dp") * rows_dev
    block = my_start // block_size
    block_start = block * block_size
    offset = my_start - block_start
    basis_block = lax.dynamic_slice_in_dim(basis_out, block, 1, 0)[0]
    eig_block = lax.dynamic_slice_in_dim(eig_out, block, 1, 0)[0]
    basis_rows = lax.dynamic_slice_in_dim(basis_block, offset, rows_dev, 0)
    summed = lax.psum(partial_grad.astype(jnp.bfloat16), "dp").astype(jnp.float32)
    block_rows = lax.dynamic_slice_in_dim(summed, block_start, block_size, 0).astype(jnp.bfloat16)
    right_side = jnp.einsum(
        "rbj,bjk->rbk",
        block_rows.reshape(block_size, local_blocks, block_size),
        basis_in,
        preferred_element_type=jnp.float32,
    ).astype(jnp.bfloat16)
    inner_term = jnp.einsum(
        "ra,rbk->abk", basis_block, right_side, preferred_element_type=jnp.float32
    )
    scaled = (inner_term / (eig_block[:, None, None] * eig_in[None, :, :] + DAMPING)).astype(
        jnp.bfloat16
    )
    upper_term = jnp.einsum(
        "ra,abk->rbk", basis_rows, scaled, preferred_element_type=jnp.float32
    ).astype(jnp.bfloat16)
    precond = jnp.einsum("rbk,bjk->rbj", upper_term, basis_in, preferred_element_type=jnp.float32)
    return (precond.reshape(rows_dev, width).astype(jnp.bfloat16), act_new, grad_new)


def solution(mesh):
    return jax.shard_map(
        per_device,
        mesh=mesh,
        in_specs=(
            P("dp", "worker"),
            P("dp", "worker"),
            P("dp"),
            P("worker", None, None),
            P(),
            P("worker", None, None),
            P("worker", None, None),
        ),
        out_specs=(P("dp", "worker"), P("worker", None, None), P("worker", None, None)),
        check_vma=False,
    )
```

profile of v0, /device:TPU:19, one launch (start us, length us, event | category | flops | bytes accessed | tf_op | source)
XLA Modules:
  0.0 513.5 jit_solution(4568117527584923640)
XLA Ops:
  7.2 0.0 copy-start
  7.2 0.0 all-gather.4.cloned.1.call-start
  7.2 0.7 all-gather.4.cloned.1.call-update
  7.9 0.0 all-reduce.3.cloned.1.call-start
  8.0 0.7 compare_select_fusion
  8.6 0.0 copy-done
  8.6 0.6 gather_fusion.1
  9.2 1.8 gather_fusion
  11.0 0.7 compare_and_fusion
  11.7 1.2 fusion.10
  12.9 1.2 fusion.11
  14.1 169.1 %all-gather.4.cloned.1.call-done = bf16[1024,4096]{1,0:T(8,128)(2,1)} async-done(((bf16[1024,512]{1,0:T(8,128)(2,1)}), bf16[1024,4096]{1,0:T(8,128)(2,1)}) %all-gather.4.cloned.1.call-update) | async-done | bytes 8388624 | tf_op jit(solution)/shard_map/all_gather | solution.py:52
  183.2 9.7 %convolution_convert_fusion = bf16[4096,512]{1,0:T(8,128)(2,1)} fusion(bf16[1024,4096]{1,0:T(8,128)(2,1)} %all-gather.4.cloned.1.call-done, bf16[1024,512]{1,0:T(8,128)(2,1)S(1)} %copy-done), kind=kOutput, calls=%fused_computation.2 | convolution fusion | flops 4297064448 | bytes 13631488 | tf_op jit(solution)/shard_map/pk,pw->kw/dot_general | solution.py:50
  192.9 0.0 all-reduce.3.cloned.1.call-update
  192.9 0.0 copy-start.1
  193.0 286.4 %all-reduce.3.cloned.1.call-done = (bf16[4096,512]{1,0:T(8,128)(2,1)}, bf16[1,512,512]{2,1,0:T(8,128)(2,1)}, bf16[1,512,512]{2,1,0:T(8,128)(2,1)}) async-done(((bf16[4096,512]{1,0:T(8,128)(2,1)}, bf16[1,512,512]{2,1,0:T(8,128)(2,1)}, bf16[1,512,512]{2,1,0:T(8,128)(2,1)}), (bf16[4096,512]{1,0:T(8,128)(2,1)}, bf16[1,512,512]{2,1,0:T(8,128)(2,1)}, bf16[1,512,512]{2,1,0:T(8,128)(2,1)})) %all-reduce.3.cloned.1.call-update) | async-done | bytes 5242896 | tf_op jit(solution)/shard_map/psum | solution.py:64
  479.4 2.2 multiply_add_fusion
  481.5 0.0 copy-start.3
  481.6 0.0 copy-start.2
  481.6 0.9 copy-done.3
  482.5 2.2 fusion.8
  484.7 16.6 %all-gather.1 = f32[8,1,512]{2,1,0:T(1,128)S(1)} all-gather(f32[1,1,512]{2,1,0:T(1,128)S(1)} %bitcast.65), channel_id=2, replica_groups=mesh['dp'=32,'worker'=8] {'worker'}, dimensions={0}, use_global_device_ids=true | all-gather | bytes 18432 | tf_op jit(solution)/shard_map/all_gather | solution.py:49
  501.4 0.0 copy-done.1
  501.4 1.0 fusion.7
  502.4 1.5 convolution_convert_fusion.1
  503.9 1.8 fusion.12
  505.7 0.0 copy-done.2
  505.7 1.0 convolution_convert_fusion.2
  (2 shorter events, 0.0 us)
Async XLA Ops:
  7.2 1.5 copy-start
  7.2 176.0 %all-gather.4.cloned.1.call-start = ((), (), s32[]{:S(2)}) async-start(), calls=%async_computation | async-start | bytes 9437184 | tf_op jit(solution)/shard_map/all_gather | solution.py:52
  7.9 471.4 %all-reduce.3.cloned.1.call-start = ((), (), s32[]{:S(2)}) async-start(), calls=%async_computation.1 | async-start | bytes 10485760 | tf_op jit(solution)/shard_map/psum | solution.py:64
  192.9 308.4 %copy-start.1 = (bf16[1,512,512]{2,1,0:T(8,128)(2,1)S(1)}, bf16[1,512,512]{2,1,0:T(8,128)(2,1)}, u32[]{:S(2)}) copy-start(bf16[1,512,512]{2,1,0:T(8,128)(2,1)} %param.12) | copy-start | bytes 1572868
  481.5 1.0 copy-start.3
  481.6 24.1 %copy-start.2 = (f32[1,512,512]{2,1,0:T(8,128)}, f32[1,512,512]{2,1,0:T(8,128)S(1)}, u32[]{:S(2)}) copy-start(f32[1,512,512]{2,1,0:T(8,128)S(1)} %get-tuple-element.7) | copy-start | bytes 3145732
Sparse Core Ops, SparseCore 0:
  9.8 173.3 all-gather.3
  193.1 286.2 all-reduce.2
where the time goes:
time: 523 us; the launch traced here: 513 us
  waiting for transfers between devices  456 us (87%)
  matrix products  19.6 us (4%)
  blocking collectives  16.6 us (3%)
  between operations  14.2 us (3%)
    psum x1, waiting for transfers between devices, per_device(): lax.psum(partial_grad.astype(jnp.bfloat16), 'dp').astype(jnp.float32)  286 us
    all_gather x1, waiting for transfers between devices, per_device(): lax.all_gather(cotan, 'worker', axis=1, tiled=True)  169 us
    all_gather x1, blocking collectives, per_device(): eig_out = lax.all_gather(eig_local, 'worker', axis=0, tiled=True)  16.6 us
  transfers between devices with their start and end apart: 2, of which 2 were waited for; matrix products, arithmetic and copies ran while one was open for 1% of the time, Pallas kernels for 0%

commit v1 on v0

v1 whole, which is shorter than its diff:
```python
import jax
import jax.numpy as jnp
from jax import lax
from jax.experimental import pallas as pl
from jax.experimental.pallas import tpu as pltpu
from jax.sharding import PartitionSpec as P

MESH = pl.DeviceIdType.MESH
DECAY_RATE = 0.75
DAMPING = 0.03
BLK = 128
NX, NY, NZ = 4, 4, 8
FB = 512
PIECE = 128
HALF = 256
NF = 8
NU = 40
BF = jnp.bfloat16
F32 = jnp.float32

BATCH = {"F": (0, 8), 0: (8, 12), 1: (12, 14), 2: (14, 16), 3: (16, 18), 4: (18, 32), 5: (32, 36), 6: (36, 40)}


def tdot(a, b):
    return lax.dot_general(a, b, (((0,), (0,)), ((), ())), preferred_element_type=F32)


def ndot(a, b):
    return lax.dot_general(a, b, (((1,), (0,)), ((), ())), preferred_element_type=F32)


def device(x, y, z, c):
    return (z * 4 + (x // 2) * 2 + c, y * 2 + x % 2)


def unit_piece(i):
    j = i - NF
    late = j >= 24
    n = jnp.where(late, 12 + ((j - 24) // 4) * 2 + j % 2, j % 12)
    e = jnp.where(late, ((j - 24) % 4) // 2, j // 12)
    return n, e


def piece_source(n):
    m = n - 4
    pair = m // 2
    far = (pair == 2) | (pair == 4)
    side = m % 2
    seq = jnp.where(pair < 2, pair, (pair + 1) // 2)
    near_q = jnp.where(side == 0, (seq + 2) % 4, seq)
    far_q = side * 2 + jnp.where(pair == 4, 1, 0)
    dy = jnp.where(far, 2, jnp.where(side == 0, 1, 3))
    q = jnp.where(far, far_q, near_q)
    own = n < 4
    return jnp.where(own, 0, dy), jnp.where(own, n, q)


def kernel(
    ids, acts, cotan, basis_in, basis_out, act_factor, grad_factor,
    precond, totals,
    cotb, actb, smp, own, cout, cin, zout, ra, rb, xr, xst, wb, ts, tr, tb, fac, ebas, bout, eigb, eigs, inner, right,
    lsem, y_ss, y_rs, x_ss, x_rs, c_ss, c_rs, z_ss, a_rs, b_rs, xs_ss, xs_rs, w_ss, w_rs, t_ss, t_rs, tx_ss, tx_rs,
    tc_ss, tc_rs, e_ss, e_rs, ec_ss, ec_rs,
):
    r = lax.axis_index("dp")
    w = lax.axis_index("worker")
    z, xh, c = r // 4, (r // 2) % 2, r % 2
    y, xl = w // 2, w % 2
    x = xh * 2 + xl
    oc = 1 - c

    def at(dx=0, dy=0, dz=0):
        return device((x + dx) % NX, (y + dy) % NY, (z + dz) % NZ, c)

    core = device(x, y, z, oc)
    zp, zm, zp2, zm2 = at(dz=1), at(dz=7), at(dz=2), at(dz=6)
    yp, ym = at(dy=1), at(dy=3)
    far_x = (1 - xh) * 2 + xl
    part_x = xh * 2 + (1 - xl)
    cross_x = (1 - xh) * 2 + (1 - xl)
    partner = device(part_x, y, z, c)
    far = device(far_x, y, z, c)
    cross = device(cross_x, y, z, c)

    def rc(src, dst, ss, rs, dev):
        return pltpu.make_async_remote_copy(
            src_ref=src, dst_ref=dst, send_sem=ss, recv_sem=rs, device_id=dev, device_id_type=MESH
        )

    loads = []
    for q in range(4):
        loads.append(pltpu.make_async_copy(cotan.at[:, pl.ds(q * PIECE, PIECE)], cotb.at[q], lsem.at[q]))
    for h in range(2):
        loads.append(pltpu.make_async_copy(acts.at[:, pl.ds(h * HALF, HALF)], actb.at[xl, h], lsem.at[4 + h]))
    loads.append(pltpu.make_async_copy(basis_out.at[z], bout, lsem.at[6]))
    for cp in loads:
        cp.start()

    @pl.when(c == 0)
    def _():
        pltpu.make_async_copy(basis_in, ebas, lsem.at[7]).start()
        pltpu.make_async_copy(act_factor, fac, lsem.at[8]).start()

    @pl.when(c == 1)
    def _():
        pltpu.make_async_copy(basis_out.at[w], ebas, lsem.at[7]).start()
        pltpu.make_async_copy(grad_factor, fac, lsem.at[8]).start()

    barrier = pltpu.get_barrier_semaphore()
    for k in range(1, 8):
        wk = (w + k) % 8
        pl.semaphore_signal(barrier, inc=1, device_id=(r, wk), device_id_type=MESH)
    for dev in (core, zp, zm, zp2, zm2, far, cross):
        pl.semaphore_signal(barrier, inc=1, device_id=dev, device_id_type=MESH)
    pl.semaphore_wait(barrier, 14)

    def send_p(k):
        return rc(cotan.at[:, pl.ds(k * PIECE, PIECE)], cotb.at[(5, 7, 11, 15)[k]], y_ss.at[k], y_rs.at[(5, 7, 11, 15)[k]], yp)

    def send_m(k):
        q = (k + 2) % 4
        return rc(cotan.at[:, pl.ds(q * PIECE, PIECE)], cotb.at[(4, 6, 10, 14)[k]], y_ss.at[4 + k], y_rs.at[(4, 6, 10, 14)[k]], ym)

    def fwd_p(k):
        src, dst = (5, 7)[k], (8, 12)[k]
        return rc(cotb.at[src], cotb.at[dst], y_ss.at[8 + k], y_rs.at[dst], yp)

    def fwd_m(k):
        src, dst = (4, 6)[k], (9, 13)[k]
        return rc(cotb.at[src], cotb.at[dst], y_ss.at[10 + k], y_rs.at[dst], ym)

    def send_x(h):
        return rc(acts.at[:, pl.ds(h * HALF, HALF)], actb.at[xl, h], x_ss.at[h], x_rs.at[h], partner)

    def recv_x(h):
        return rc(acts.at[:, pl.ds(h * HALF, HALF)], actb.at[1 - xl, h], x_ss.at[h], x_rs.at[h], partner)

    for k in range(2):
        send_p(k).start()
        send_m(k).start()
        send_x(k).start()

    def wait_piece(n):
        rc(cotb.at[n], cotb.at[n], y_ss.at[0], y_rs.at[n], yp).wait_recv()

    for cp in loads[:6]:
        cp.wait()

    def target(i):
        n, _ = unit_piece(i)
        dy, _ = piece_source(n)
        return jnp.where(i < NF, i, 2 * ((y + dy) % NY) + xl)

    def dist(i):
        return (target(i) - z + NZ) % NZ

    def core_copy(i):
        return rc(cout.at[i], cin.at[i], c_ss.at[i], c_rs.at[i], core)

    def z_copy(i, dev, land, sem):
        return rc(zout.at[i], land.at[i], z_ss.at[i], sem.at[i], dev)

    def recv_a(i):
        z_copy(i, zp, ra, a_rs).wait_recv()

    def recv_b(i):
        z_copy(i, zm, rb, b_rs).wait_recv()

    def compute_factor():
        scale_own = jnp.where(c == 0, 1.0 / 8192, 4.0).astype(F32)
        scale_other = jnp.where(c == 0, 4.0, 1.0 / 8192).astype(F32)
        for s in range(2):
            into = slice(s * BLK, (s + 1) * BLK)
            for h in range(2):
                block = actb[xl, h, :BLK, :]
                for k in range(1, 8):
                    block = jnp.where(ids[s] == k, actb[xl, h, k * BLK : (k + 1) * BLK, :], block)
                smp[0, into, h * HALF : (h + 1) * HALF] = block
            for q in range(4):
                block = cotb[q, :BLK, :]
                for k in range(1, 8):
                    block = jnp.where(ids[s] == k, cotb[q, k * BLK : (k + 1) * BLK, :], block)
                smp[1, into, q * PIECE : (q + 1) * PIECE] = block

        @pl.loop(0, NF)
        def _(i):
            left = pl.ds(pl.multiple_of((i // 2) * PIECE, PIECE), PIECE)
            cols = pl.ds(pl.multiple_of((i % 2) * HALF, HALF), HALF)
            cout[i] = (tdot(smp[oc, :, left], smp[oc, :, cols]) * scale_other).astype(BF)
            core_copy(i).start()
            own[i] = tdot(smp[c, :, left], smp[c, :, cols]) * scale_own

    def compute(lo, hi):
        @pl.loop(lo, hi)
        def _(i):
            n, e = unit_piece(i)
            ea = jnp.where(e == 0, xl, 1 - xl)
            cout[i] = tdot(cotb[n], actb[ea, oc]).astype(BF)
            core_copy(i).start()
            own[i] = tdot(cotb[n], actb[ea, c])

    def merge(batch):
        lo, hi = BATCH[batch]

        @pl.loop(lo, hi)
        def _(i):
            core_copy(i).wait_recv()
            acc = own[i] + cin[i].astype(F32)
            own[i] = acc
            d = dist(i)

            @pl.when((d == 4) | (d == 5))
            def _():
                zout[i] = acc.astype(BF)

            @pl.when(d == 4)
            def _():
                z_copy(i, zp, ra, a_rs).start()

            @pl.when(d == 5)
            def _():
                z_copy(i, zm, rb, b_rs).start()

    def hop(batch, lag):
        lo, hi = BATCH[batch]

        @pl.loop(lo, hi)
        def _(i):
            d = dist(i)
            if lag < 4:
                @pl.when(d == 4 - lag)
                def _():
                    recv_a(i)
                    zout[i] = (own[i] + ra[i].astype(F32)).astype(BF)
                    z_copy(i, zp, ra, a_rs).start()

            if lag < 3:
                @pl.when(d == 5 + lag)
                def _():
                    recv_b(i)
                    zout[i] = (own[i] + rb[i].astype(F32)).astype(BF)
                    z_copy(i, zm, rb, b_rs).start()

            if lag == 4:
                @pl.when(d == 0)
                def _():
                    recv_a(i)
                    recv_b(i)
                    total = (own[i] + ra[i].astype(F32) + rb[i].astype(F32)).astype(BF)
                    if batch == "F":
                        ts[...] = total
                        rc(ts, tr, tx_ss.at[0], tx_rs.at[0], far).start()
                    else:
                        n, e = unit_piece(i)
                        _, q = piece_source(n)

                        @pl.when(e == 0)
                        def _():
                            xr[xh, q] = total
                            rc(xr.at[xh, q], xr.at[xh, q], xs_ss.at[0, q], xs_rs.at[xh, q], far).start()

                        @pl.when(e == 1)
                        def _():
                            xst[q] = total
                            rc(xst.at[q], xr.at[xh, q], xs_ss.at[1, q], xs_rs.at[xh, q], partner).start()
                            rc(xst.at[q], xr.at[xh, q], xs_ss.at[2, q], xs_rs.at[xh, q], cross).start()

    def t_copy(o, k, dev):
        return rc(tb.at[c, o], tb.at[c, o], t_ss.at[k], t_rs.at[o], dev)

    def t_core(o):
        return rc(tb.at[c, o], tb.at[c, o], tc_ss.at[o], tc_rs.at[o], core)

    def t_core_recv(o):
        return rc(tb.at[oc, o], tb.at[oc, o], tc_ss.at[o], tc_rs.at[o], core)

    def origin(dz):
        return (z + dz) % NZ

    def spread_1():
        rc(ts, tr, tx_ss.at[0], tx_rs.at[0], far).wait_recv()
        tb[c, z] = (ts[...].astype(F32) + tr[...].astype(F32)).astype(BF)
        for k, dev in enumerate((zp, zm, zp2, zm2)):
            t_copy(z, k, dev).start()
        t_core(z).start()

    def t_arrived(dz):
        o = origin(dz)
        t_copy(o, 0, zp).wait_recv()
        t_core(o).start()

    def spread_2():
        t_arrived(6)
        t_copy(origin(6), 4, zp).start()
        t_copy(origin(6), 5, zp2).start()
        t_arrived(2)
        t_copy(origin(2), 6, zm).start()
        t_arrived(7)
        t_arrived(1)

    def spread_3():
        t_arrived(5)
        t_arrived(3)
        t_arrived(4)

    def eigen():
        pltpu.make_async_copy(act_factor, fac, lsem.at[8]).wait()
        pltpu.make_async_copy(basis_in, ebas, lsem.at[7]).wait()
        eigs[...] = jnp.zeros_like(eigs)

        @pl.loop(0, 4)
        def _(q):
            rows = pl.ds(pl.multiple_of(q * PIECE, PIECE), PIECE)
            prod = jnp.zeros((PIECE, FB), F32)
            for h in range(2):
                new = (
                    DECAY_RATE * fac[rows, h * HALF : (h + 1) * HALF]
                    + (1.0 - DECAY_RATE) * tb[c, 2 * q + h].astype(F32)
                )
                basis = ebas[h * HALF : (h + 1) * HALF, :]
                for _ in range(3):
                    part = new.astype(BF)
                    prod = prod + ndot(part, basis)
                    new = new - part.astype(F32)
            prod = prod * ebas[rows, :].astype(F32)
            eigs[...] += jnp.sum(prod.reshape(PIECE // 8, 8, FB), axis=0)

        eig = jnp.broadcast_to(jnp.sum(eigs[...], axis=0, keepdims=True), (8, FB))

        @pl.when(c == 0)
        def _():
            eigb[0] = eig
            rc(eigb.at[0], eigb.at[0], ec_ss, ec_rs, core).start()

        @pl.when((c == 1) & (w == z))
        def _():
            eigb[1] = eig
            for k in range(1, 8):
                rc(eigb.at[1], eigb.at[1], e_ss.at[k - 1], e_rs, (r, (w + k) % 8)).start()

    def eigen_pass():
        @pl.when(c == 1)
        def _():
            @pl.when(w != z)
            def _():
                rc(eigb.at[1], eigb.at[1], e_ss.at[0], e_rs, (r, z)).wait_recv()

            rc(eigb.at[1], eigb.at[1], ec_ss, ec_rs, core).start()

    compute_factor()
    merge("F")
    compute(*BATCH[0])
    merge(0)
    hop("F", 1)
    wait_piece(5)
    fwd_p(0).start()
    send_p(2).start()
    wait_piece(4)
    fwd_m(0).start()
    send_m(2).start()
    compute(*BATCH[1])
    hop("F", 2)
    hop(0, 1)
    merge(1)
    hop("F", 3)
    wait_piece(7)
    fwd_p(1).start()
    send_p(3).start()
    wait_piece(6)
    fwd_m(1).start()
    send_m(3).start()
    compute(*BATCH[2])
    hop("F", 4)
    hop(0, 2)
    hop(1, 1)
    merge(2)
    spread_1()
    wait_piece(8)
    wait_piece(9)
    compute(*BATCH[3])
    hop(0, 3)
    hop(1, 2)
    hop(2, 1)
    merge(3)
    spread_2()
    recv_x(0).wait_recv()
    recv_x(1).wait_recv()
    wait_piece(11)
    wait_piece(10)
    hop(0, 4)
    hop(1, 3)
    hop(2, 2)
    hop(3, 1)
    compute(*BATCH[4])
    merge(4)
    spread_3()
    wait_piece(12)
    wait_piece(13)
    hop(1, 4)
    hop(2, 3)
    hop(3, 2)
    hop(4, 1)
    compute(*BATCH[5])
    merge(5)
    eigen()
    wait_piece(15)
    wait_piece(14)
    compute(*BATCH[6])
    hop(2, 4)
    hop(3, 3)
    hop(4, 2)
    hop(5, 1)
    merge(6)
    eigen_pass()
    hop(3, 4)
    hop(4, 3)
    hop(5, 2)
    hop(6, 1)
    for o in range(NF):
        t_core_recv(o).wait_recv()
    for f in range(2):
        for o in range(NF):
            pltpu.make_async_copy(
                tb.at[f, o],
                totals.at[f, pl.ds((o // 2) * PIECE, PIECE), pl.ds((o % 2) * HALF, HALF)],
                lsem.at[9 + f * NF + o],
            ).start()
    hop(4, 4)
    hop(5, 3)
    hop(6, 2)
    hop(5, 4)
    hop(6, 3)
    hop(6, 4)

    pltpu.make_async_copy(basis_out.at[z], bout, lsem.at[6]).wait()
    inner[...] = jnp.zeros_like(inner)

    def w_copy(h, q):
        return rc(wb.at[h, q], wb.at[h, q], w_ss.at[q], w_rs.at[q], core)

    home = (z % 2) == xl

    @pl.loop(0, 4)
    def _(q):
        @pl.when(jnp.logical_not(home))
        def _():
            rc(xst.at[q], xr.at[xh, q], xs_ss.at[0, q], xs_rs.at[xh, q], far).wait_recv()

        rc(xst.at[q], xr.at[1 - xh, q], xs_ss.at[0, q], xs_rs.at[1 - xh, q], far).wait_recv()
        wb[c, q] = (xr[0, q].astype(F32) + xr[1, q].astype(F32)).astype(BF)
        w_copy(c, q).start()

    @pl.loop(0, 4)
    def _(q):
        w_copy(oc, q).wait_recv()
        right[...] = (ndot(wb[0, q], basis_in[:HALF, :]) + ndot(wb[1, q], basis_in[HALF:, :])).astype(BF)
        rows = pl.ds(pl.multiple_of(q * PIECE, PIECE), PIECE)
        inner[...] += tdot(bout[rows, :], right[...])

    @pl.when(c == 0)
    def _():
        rc(eigb.at[1], eigb.at[1], ec_ss, ec_rs, core).wait_recv()

    @pl.when(c == 1)
    def _():
        rc(eigb.at[0], eigb.at[0], ec_ss, ec_rs, core).wait_recv()

    ei = eigb[0, 0:1, :]
    eo = jnp.transpose(jnp.broadcast_to(eigb[1, 0:1, :], (PIECE, FB)))
    eo = jnp.concatenate([eo] * 4, axis=1)
    scaled = (inner[...] / (eo * ei + DAMPING)).astype(BF)
    mine = pl.ds(pl.multiple_of((xh * 2 + c) * PIECE, PIECE), PIECE)
    upper = ndot(bout[mine, :], scaled).astype(BF)
    precond[...] = lax.dot_general(
        upper, basis_in[...], (((1,), (1,)), ((), ())), preferred_element_type=F32
    ).astype(BF)

    for k in range(4):
        send_p(k).wait_send()
        send_m(k).wait_send()
    for k in range(2):
        fwd_p(k).wait_send()
        fwd_m(k).wait_send()
        send_x(k).wait_send()

    @pl.loop(0, NU)
    def _(i):
        core_copy(i).wait_send()

        @pl.when(dist(i) != 0)
        def _():
            z_copy(i, zp, ra, a_rs).wait_send()

    rc(ts, tr, tx_ss.at[0], tx_rs.at[0], far).wait_send()
    for k in range(7):
        t_copy(z, k, zp).wait_send()
    for o in range(NF):
        t_core(o).wait_send()

    @pl.when(home)
    def _():
        for k in range(3):
            for q in range(4):
                rc(xst.at[q], xr.at[xh, q], xs_ss.at[k, q], xs_rs.at[xh, q], far).wait_send()

    for q in range(4):
        w_copy(c, q).wait_send()
    rc(eigb.at[0], eigb.at[0], ec_ss, ec_rs, core).wait_send()

    @pl.when((c == 1) & (w == z))
    def _():
        for k in range(1, 8):
            rc(eigb.at[1], eigb.at[1], e_ss.at[k - 1], e_rs, (r, (w + k) % 8)).wait_send()

    for f in range(2):
        for o in range(NF):
            pltpu.make_async_copy(
                tb.at[f, o],
                totals.at[f, pl.ds((o // 2) * PIECE, PIECE), pl.ds((o % 2) * HALF, HALF)],
                lsem.at[9 + f * NF + o],
            ).wait()


def per_device(acts, cotan, block_ids, basis_in, basis_out, act_factor, grad_factor):
    vm = pltpu.VMEM
    dma = pltpu.SemaphoreType.DMA
    unit = (PIECE, HALF)
    any_spec = pl.BlockSpec(memory_space=pl.ANY)
    precond, totals = pl.pallas_call(
        kernel,
        name="kfac",
        out_shape=(
            jax.ShapeDtypeStruct((PIECE, FB), BF),
            jax.ShapeDtypeStruct((2, FB, FB), BF),
        ),
        in_specs=[
            pl.BlockSpec(memory_space=pltpu.SMEM),
            any_spec,
            any_spec,
            pl.BlockSpec(memory_space=pltpu.VMEM),
            any_spec,
            any_spec,
            any_spec,
        ],
        out_specs=(pl.BlockSpec(memory_space=pltpu.VMEM), any_spec),
        scratch_shapes=[
            vm((16, 1024, PIECE), BF),
            vm((2, 2, 1024, HALF), BF),
            vm((2, 2 * BLK, FB), BF),
            vm((NU,) + unit, F32),
            vm((NU,) + unit, BF),
            vm((NU,) + unit, BF),
            vm((NU,) + unit, BF),
            vm((NU,) + unit, BF),
            vm((NU,) + unit, BF),
            vm((2, 4) + unit, BF),
            vm((4,) + unit, BF),
            vm((2, 4) + unit, BF),
            vm(unit, BF),
            vm(unit, BF),
            vm((2, NF) + unit, BF),
            vm((FB, FB), F32),
            vm((FB, FB), BF),
            vm((FB, FB), BF),
            vm((2, 8, FB), F32),
            vm((8, FB), F32),
            vm((FB, FB), F32),
            vm((PIECE, FB), BF),
            dma((25,)),
            dma((12,)),
            dma((16,)),
            dma((2,)),
            dma((2,)),
            dma((NU,)),
            dma((NU,)),
            dma((NU,)),
            dma((NU,)),
            dma((NU,)),
            dma((3, 4)),
            dma((2, 4)),
            dma((4,)),
            dma((4,)),
            dma((7,)),
            dma((NF,)),
            dma((1,)),
            dma((1,)),
            dma((NF,)),
            dma((NF,)),
            dma((7,)),
            dma,
            dma,
            dma,
        ],
        compiler_params=pltpu.CompilerParams(
            collective_id=0, has_side_effects=True, vmem_limit_bytes=48 << 20
        ),
    )(
        block_ids,
        acts,
        cotan,
        basis_in.reshape(FB, FB),
        basis_out,
        act_factor.reshape(FB, FB),
        grad_factor.reshape(FB, FB),
    )
    totals = totals.astype(F32)
    act_new = DECAY_RATE * act_factor + (1.0 - DECAY_RATE) * totals[0:1]
    grad_new = DECAY_RATE * grad_factor + (1.0 - DECAY_RATE) * totals[1:2]
    return precond, act_new, grad_new


def solution(mesh):
    return jax.shard_map(
        per_device,
        mesh=mesh,
        in_specs=(
            P("dp", "worker"),
            P("dp", "worker"),
            P("dp"),
            P("worker", None, None),
            P(),
            P("worker", None, None),
            P("worker", None, None),
        ),
        out_specs=(P("dp", "worker"), P("worker", None, None), P("worker", None, None)),
        check_vma=False,
    )
```

time: 523 us -> 118 us (0.23)
  the two profiles are of different devices: /device:TPU:19 before, /device:TPU:57 now
where the time goes in v1:
time: 118 us
  Pallas kernels  108 us (92%)
  local copies, waits for them, and re-layouts  7.24 us (6%)
  other arithmetic  2.1 us (2%)
    pallas_call x1, Pallas kernels, per_device(): pl.pallas_call(kernel, name='kfac', out_shape=(jax.ShapeDtypeStruct((PIEC...  108 us
    unnamed x13, local copies, waits for them, and re-layouts  7.24 us

profile of v1, /device:TPU:57, one launch (start us, length us, event | category | flops | bytes accessed | tf_op | source)
XLA Modules:
  0.0 117.7 jit_solution(11846946236252813735)
XLA Ops:
  0.6 0.0 copy-start
  0.6 1.2 %copy-done = f32[1,512,512]{2,1,0:T(8,128)S(1)} copy-done((f32[1,512,512]{2,1,0:T(8,128)S(1)}, f32[1,512,512]{2,1,0:T(8,128)}, u32[]{:S(2)}) %copy-start) | copy-done | bytes 1048600
  1.9 0.0 copy-start.1
  1.9 1.2 %copy-done.1 = f32[1,512,512]{2,1,0:T(8,128)S(1)} copy-done((f32[1,512,512]{2,1,0:T(8,128)S(1)}, f32[1,512,512]{2,1,0:T(8,128)}, u32[]{:S(2)}) %copy-start.1) | copy-done | bytes 1048600
  3.1 0.0 copy-start.2
  3.1 1.2 %copy-done.2 = bf16[1024,512]{1,0:T(8,128)(2,1)S(1)} copy-done((bf16[1024,512]{1,0:T(8,128)(2,1)S(1)}, bf16[1024,512]{1,0:T(8,128)(2,1)}, u32[]{:S(2)}) %copy-start.2) | copy-done | bytes 1048600
  4.3 0.0 copy-start.3
  4.3 1.2 %copy-done.3 = bf16[1024,512]{1,0:T(8,128)(2,1)S(1)} copy-done((bf16[1024,512]{1,0:T(8,128)(2,1)S(1)}, bf16[1024,512]{1,0:T(8,128)(2,1)}, u32[]{:S(2)}) %copy-start.3) | copy-done | bytes 1048600
  5.5 0.0 copy-start.4
  5.5 1.0 copy-done.4
  6.6 0.0 copy-start.5
  6.6 0.7 copy-done.5
  7.2 107.7 %kfac.1 = (bf16[128,512]{1,0:T(8,128)(2,1)S(1)}, bf16[2,512,512]{2,1,0:T(8,128)(2,1)S(1)}) custom-call(s32[2]{0:T(128)S(1)} %copy-done.5, bf16[1024,512]{1,0:T(8,128)(2,1)S(1)} %copy-done.2, bf16[1024,512]{1,0:T(8,128)(2,1)S(1)} %copy-done.3, bf16[512,512]{1,0:T(8,128)(2,1)S(1)} %bitcast.5, bf16[8,512,512]{2,1,0:T(8,128)(2,1)} %basis_out.1, ...), custom_call_target="tpu_custom_call" | custom-call | tf_op jit(solution)/shard_map/kfac/pallas_call | solution.py:529
  114.9 0.3 convert_element_type.3
  115.2 1.8 %fusion = (f32[1,512,512]{2,1,0:T(8,128)}, f32[1,512,512]{2,1,0:T(8,128)}) fusion(f32[2,512,512]{2,1,0:T(8,128)S(1)} %convert_element_type.3, f32[1,512,512]{2,1,0:T(8,128)S(1)} %copy-done.1, f32[1,512,512]{2,1,0:T(8,128)S(1)} %copy-done), kind=kLoop, calls=%fused_computation.1 | loop fusion | flops 1572864 | bytes 6291456 | tf_op jit(solution)/shard_map/add | solution.py:608
  117.0 0.7 copy.11
Async XLA Ops:
  0.6 1.2 %copy-start = (f32[1,512,512]{2,1,0:T(8,128)S(1)}, f32[1,512,512]{2,1,0:T(8,128)}, u32[]{:S(2)}) copy-start(f32[1,512,512]{2,1,0:T(8,128)} %param.12) | copy-start | bytes 3145732
  1.9 1.2 %copy-start.1 = (f32[1,512,512]{2,1,0:T(8,128)S(1)}, f32[1,512,512]{2,1,0:T(8,128)}, u32[]{:S(2)}) copy-start(f32[1,512,512]{2,1,0:T(8,128)} %param.13) | copy-start | bytes 3145732
  3.1 1.2 %copy-start.2 = (bf16[1024,512]{1,0:T(8,128)(2,1)S(1)}, bf16[1024,512]{1,0:T(8,128)(2,1)}, u32[]{:S(2)}) copy-start(bf16[1024,512]{1,0:T(8,128)(2,1)} %acts.1) | copy-start | bytes 3145732
  4.3 1.2 %copy-start.3 = (bf16[1024,512]{1,0:T(8,128)(2,1)S(1)}, bf16[1024,512]{1,0:T(8,128)(2,1)}, u32[]{:S(2)}) copy-start(bf16[1024,512]{1,0:T(8,128)(2,1)} %cotan.1) | copy-start | bytes 3145732
  5.5 1.0 copy-start.4
  6.6 0.7 copy-start.5

commit v2 on v1

v2 whole, which is shorter than its diff:
```python
import jax
import jax.numpy as jnp
from jax import lax
from jax.experimental import pallas as pl
from jax.experimental.pallas import tpu as pltpu
from jax.sharding import PartitionSpec as P

MESH = pl.DeviceIdType.MESH
DECAY_RATE = 0.75
DAMPING = 0.03
BLK = 128
NX, NY, NZ = 4, 4, 8
FB = 512
PIECE = 128
HALF = 256
NF = 8
NU = 40
TREE_FROM = 40
BF = jnp.bfloat16
F32 = jnp.float32


def tdot(a, b):
    return lax.dot_general(a, b, (((0,), (0,)), ((), ())), preferred_element_type=F32)


def ndot(a, b):
    return lax.dot_general(a, b, (((1,), (0,)), ((), ())), preferred_element_type=F32)


def device(x, y, z, c):
    return (z * 4 + (x // 2) * 2 + c, y * 2 + x % 2)


def unit_parts(i):
    j = i - NF
    runs = (
        (0, 0, 0, None),
        (8, 0, 1, 0),
        (12, 4, 0, None),
        (14, 4, 1, 0),
        (15, 5, 0, None),
        (17, 5, 1, 0),
        (18, 0, 1, 1),
    )
    m, e, h = j, j, j
    for lo, pair, acts, half in runs:
        here = j >= lo
        m = jnp.where(here, pair + ((j - lo) // 2 if half is None else j - lo), m)
        e = jnp.where(here, acts, e)
        h = jnp.where(here, (j - lo) % 2 if half is None else half, h)
    late = j >= 24
    m = jnp.where(late, 6 + (j - 24) // 4, m)
    e = jnp.where(late, (j // 2) % 2, e)
    h = jnp.where(late, j % 2, h)
    return m, e, h


def kept_piece(m, c):
    return 2 * m + jnp.where((m == 3) | (m == 7), 1 - c, c)


def piece_source(n):
    m = n // 2
    far = (m == 4) | (m == 6)
    k = jnp.where(m < 2, 0, jnp.where(far, 3, 1 + n % 2))
    far_idx = jnp.where(m == 6, 2, 0) + n % 2
    idx = jnp.where(m < 2, n, jnp.where(far, far_idx, jnp.where(m < 4, m - 2, (m - 1) // 2)))
    return k, idx


def feature_block(k, idx):
    return jnp.where(k == 3, (idx % 2) * 2 + idx // 2, jnp.where(k == 1, (idx + 2) % 4, idx))


def y_offset(k):
    return jnp.where(k == 2, 3, jnp.where(k == 3, 2, k))


def kernel(
    ids, acts, cotan, basis_in, basis_out, act_factor, grad_factor,
    precond, act_new, grad_new,
    cotb, actb, smp, own, cout, cin, zout, ra, rb, rcc, rd, xr, xst, wb, ts, tr, tb, fac, ebas, bout, eigb, eigs, scaled, right,
    lsem, y_ss, y_rs, x_ss, x_rs, c_ss, c_rs, z_ss, a_rs, b_rs, cc_rs, d_rs, xs_ss, xs_rs, w_ss, w_rs, t_ss, t_rs, tx_ss, tx_rs,
    tc_ss, tc_rs, e_ss, e_rs, ec_ss, ec_rs,
):
    r = lax.axis_index("dp")
    w = lax.axis_index("worker")
    z, xh, c = r // 4, (r // 2) % 2, r % 2
    y, xl = w // 2, w % 2
    x = xh * 2 + xl
    oc = 1 - c

    def at(dx=0, dy=0, dz=0):
        return device((x + dx) % NX, (y + dy) % NY, (z + dz) % NZ, c)

    core = device(x, y, z, oc)
    zp, zm, zp2, zm2 = at(dz=1), at(dz=7), at(dz=2), at(dz=6)
    yp, ym = at(dy=1), at(dy=3)
    far_x = (1 - xh) * 2 + xl
    part_x = xh * 2 + (1 - xl)
    cross_x = (1 - xh) * 2 + (1 - xl)
    partner = device(part_x, y, z, c)
    far = device(far_x, y, z, c)
    cross = device(cross_x, y, z, c)

    def rc(src, dst, ss, rs, dev):
        return pltpu.make_async_remote_copy(
            src_ref=src, dst_ref=dst, send_sem=ss, recv_sem=rs, device_id=dev, device_id_type=MESH
        )

    loads = []
    for q in range(4):
        into = cotb.at[q // 2, :, pl.ds((q % 2) * PIECE, PIECE)]
        loads.append(pltpu.make_async_copy(cotan.at[:, pl.ds(q * PIECE, PIECE)], into, lsem.at[q]))
    for h in range(2):
        loads.append(pltpu.make_async_copy(acts.at[:, pl.ds(h * HALF, HALF)], actb.at[xl, h], lsem.at[4 + h]))
    loads.append(pltpu.make_async_copy(basis_out.at[z], bout, lsem.at[6]))
    for cp in loads:
        cp.start()

    @pl.when(c == 0)
    def _():
        pltpu.make_async_copy(basis_in, ebas, lsem.at[7]).start()

    @pl.when(c == 1)
    def _():
        pltpu.make_async_copy(basis_out.at[w], ebas, lsem.at[7]).start()

    factor_loads = [
        pltpu.make_async_copy(act_factor, fac.at[0], lsem.at[8]),
        pltpu.make_async_copy(grad_factor, fac.at[1], lsem.at[9]),
    ]
    for cp in factor_loads:
        cp.start()

    barrier = pltpu.get_barrier_semaphore()
    for k in range(1, 8):
        wk = (w + k) % 8
        pl.semaphore_signal(barrier, inc=1, device_id=(r, wk), device_id_type=MESH)
    for dev in (core, zp, zm, zp2, zm2, far, cross):
        pl.semaphore_signal(barrier, inc=1, device_id=dev, device_id_type=MESH)
    pl.semaphore_wait(barrier, 14)

    def piece(n):
        return cotb.at[n // 2, :, pl.ds((n % 2) * PIECE, PIECE)]

    def send_p(k):
        n = (5, 7, 11, 15)[k]
        return rc(cotan.at[:, pl.ds(k * PIECE, PIECE)], piece(n), y_ss.at[k], y_rs.at[n], yp)

    def send_m(k):
        n = (4, 6, 10, 14)[k]
        q = (k + 2) % 4
        return rc(cotan.at[:, pl.ds(q * PIECE, PIECE)], piece(n), y_ss.at[4 + k], y_rs.at[n], ym)

    def fwd_p(k):
        src, dst = (5, 7)[k], (8, 12)[k]
        return rc(piece(src), piece(dst), y_ss.at[8 + k], y_rs.at[dst], yp)

    def fwd_m(k):
        src, dst = (4, 6)[k], (9, 13)[k]
        return rc(piece(src), piece(dst), y_ss.at[10 + k], y_rs.at[dst], ym)

    def send_x(h):
        return rc(acts.at[:, pl.ds(h * HALF, HALF)], actb.at[xl, h], x_ss.at[h], x_rs.at[h], partner)

    def recv_x(h):
        return rc(acts.at[:, pl.ds(h * HALF, HALF)], actb.at[1 - xl, h], x_ss.at[h], x_rs.at[h], partner)

    for k in range(2):
        send_p(k).start()
        send_m(k).start()
        send_x(k).start()

    def wait_piece(n):
        rc(piece(n), piece(n), y_ss.at[0], y_rs.at[n], yp).wait_recv()

    for cp in loads[:6]:
        cp.wait()

    def dist(i):
        k, _ = piece_source(kept_piece(unit_parts(i)[0], c))
        to = jnp.where(i < NF, i, 2 * ((y + y_offset(k)) % NY) + xl)
        return (to - z + NZ) % NZ

    def core_copy(i):
        return rc(cout.at[i], cin.at[i], c_ss.at[i], c_rs.at[i], core)

    def z_copy(i, dev, land, sem):
        return rc(zout.at[i], land.at[i], z_ss.at[i], sem.at[i], dev)

    lands = {"a": (ra, a_rs), "b": (rb, b_rs), "c": (rcc, cc_rs), "d": (rd, d_rs)}

    def send_z(i, dev, slot):
        z_copy(i, dev, *lands[slot]).start()

    def recv_z(i, slots):
        for slot in slots:
            z_copy(i, zp, *lands[slot]).wait_recv()
        acc = own[i]
        for slot in slots:
            acc = acc + lands[slot][0][i].astype(F32)
        return acc.astype(BF)

    def compute_factor():
        scale_own = jnp.where(c == 0, 1.0 / 8192, 4.0).astype(F32)
        scale_other = jnp.where(c == 0, 4.0, 1.0 / 8192).astype(F32)
        for s in range(2):
            into = slice(s * BLK, (s + 1) * BLK)
            for h in range(2):
                block = actb[xl, h, :BLK, :]
                for k in range(1, 8):
                    block = jnp.where(ids[s] == k, actb[xl, h, k * BLK : (k + 1) * BLK, :], block)
                smp[0, into, h * HALF : (h + 1) * HALF] = block
            for q in range(4):
                cols = slice((q % 2) * PIECE, (q % 2 + 1) * PIECE)
                block = cotb[q // 2, :BLK, cols]
                for k in range(1, 8):
                    block = jnp.where(ids[s] == k, cotb[q // 2, k * BLK : (k + 1) * BLK, cols], block)
                smp[1, into, q * PIECE : (q + 1) * PIECE] = block

        @pl.loop(0, NF)
        def _(i):
            left = pl.ds(pl.multiple_of((i // 2) * PIECE, PIECE), PIECE)
            cols = pl.ds(pl.multiple_of((i % 2) * HALF, HALF), HALF)
            cout[i] = (tdot(smp[oc, :, left], smp[oc, :, cols]) * scale_other).astype(BF)
            core_copy(i).start()
            own[i] = tdot(smp[c, :, left], smp[c, :, cols]) * scale_own

    def compute(i):
        m, e, h = unit_parts(i)
        ea = jnp.where(e == 0, xl, 1 - xl)
        both = tdot(cotb[m], actb[ea, h])
        lower = kept_piece(m, c) % 2 == 0
        cout[i] = jnp.where(lower, both[PIECE:], both[:PIECE]).astype(BF)
        core_copy(i).start()
        own[i] = jnp.where(lower, both[:PIECE], both[PIECE:])

    def is_tree(i):
        return (i >= TREE_FROM) | (i < NF)

    def merge(i):
        core_copy(i).wait_recv()
        acc = own[i] + cin[i].astype(F32)
        own[i] = acc
        d = dist(i)
        tree = is_tree(i)
        far_up = d == 4
        far_down = d == 5
        near_up = tree & ((d == 1) | (d == 3))
        near_down = tree & (d == 7)

        @pl.when(far_up | far_down | near_up | near_down)
        def _():
            zout[i] = acc.astype(BF)

        @pl.when(far_up & tree)
        def _():
            send_z(i, zp2, "a")

        @pl.when((far_up & jnp.logical_not(tree)) | (near_up & (d == 1)))
        def _():
            send_z(i, zp, "a")

        @pl.when(near_up & (d == 3))
        def _():
            send_z(i, zp, "b")

        @pl.when(far_down | near_down)
        def _():
            send_z(i, zm, "b")

    def pass_on(i, cond, slots, dev, slot):
        @pl.when(cond)
        def _():
            zout[i] = recv_z(i, slots)
            send_z(i, dev, slot)

    def finish_z(i, cond, slots):
        @pl.when(cond)
        def _():
            total = recv_z(i, slots)

            @pl.when(i < NF)
            def _():
                ts[...] = total
                rc(ts, tr, tx_ss.at[0], tx_rs.at[0], far).start()

            @pl.when(i >= NF)
            def _():
                m, e, h = unit_parts(i)
                q = feature_block(*piece_source(kept_piece(m, c)))

                @pl.when(e == 0)
                def _():
                    xr[xh, q, h] = total
                    rc(xr.at[xh, q, h], xr.at[xh, q, h], xs_ss.at[0, q, h], xs_rs.at[xh, q, h], far).start()

                @pl.when(e == 1)
                def _():
                    xst[q, h] = total
                    rc(xst.at[q, h], xr.at[xh, q, h], xs_ss.at[1, q, h], xs_rs.at[xh, q, h], partner).start()
                    rc(xst.at[q, h], xr.at[xh, q, h], xs_ss.at[2, q, h], xs_rs.at[xh, q, h], cross).start()

    def hop_1(i):
        d, tree = dist(i), is_tree(i)
        chain = jnp.logical_not(tree)
        pass_on(i, (d == 3) & chain, "a", zp, "a")
        pass_on(i, (d == 6) & chain, "b", zm, "b")
        pass_on(i, (d == 2) & tree, "ab", zp2, "c")
        pass_on(i, (d == 6) & tree, "b", zm2, "d")

    def hop_2(i):
        d, tree = dist(i), is_tree(i)
        chain = jnp.logical_not(tree)
        pass_on(i, (d == 2) & chain, "a", zp, "a")
        pass_on(i, (d == 7) & chain, "b", zm, "b")
        finish_z(i, (d == 0) & tree, "abcd")

    def hop_3(i):
        pass_on(i, (dist(i) == 1) & jnp.logical_not(is_tree(i)), "a", zp, "a")

    def hop_4(i):
        finish_z(i, (dist(i) == 0) & jnp.logical_not(is_tree(i)), "ab")

    stages = (compute, merge, hop_1, hop_2, hop_3, hop_4)
    done = [NF] * len(stages)

    def advance(stage, to):
        lo, to = done[stage], min(to, NU)
        if to > lo:
            pl.loop(lo, to)(stages[stage])
            done[stage] = to

    def advance_all(to, lags):
        for stage in range(len(stages) - 1, 0, -1):
            advance(stage, to - lags[stage])

    def run(to, lags):
        lo = done[0]
        advance_all(lo, lags)

        @pl.loop(lo, to)
        def _(i):
            compute(i)
            for stage in range(1, len(stages)):
                first, lag = done[stage], lags[stage]
                if to - lag > first:
                    if lo - lag >= first:
                        stages[stage](i - lag)
                    else:
                        pl.when(i - lag >= first)(lambda stage=stage, lag=lag: stages[stage](i - lag))

        done[0] = to
        for stage in range(1, len(stages)):
            done[stage] = max(done[stage], to - lags[stage])

    def each_factor(step):
        pl.loop(0, NF)(step)

    def t_copy(o, k, dev):
        return rc(tb.at[c, o], tb.at[c, o], t_ss.at[k], t_rs.at[o], dev)

    def t_core(o):
        return rc(tb.at[c, o], tb.at[c, o], tc_ss.at[o], tc_rs.at[o], core)

    def t_core_recv(o):
        return rc(tb.at[oc, o], tb.at[oc, o], tc_ss.at[o], tc_rs.at[o], core)

    def origin(dz):
        return (z + dz) % NZ

    def spread_1():
        rc(ts, tr, tx_ss.at[0], tx_rs.at[0], far).wait_recv()
        tb[c, z] = (ts[...].astype(F32) + tr[...].astype(F32)).astype(BF)
        for k, dev in enumerate((zp, zm, zp2, zm2)):
            t_copy(z, k, dev).start()
        t_core(z).start()

    def t_arrived(dz):
        o = origin(dz)
        t_copy(o, 0, zp).wait_recv()
        t_core(o).start()

    def spread_2():
        t_arrived(6)
        t_copy(origin(6), 4, zp).start()
        t_copy(origin(6), 5, zp2).start()
        t_arrived(2)
        t_copy(origin(2), 6, zm).start()
        t_arrived(7)
        t_arrived(1)

    def spread_3():
        t_arrived(5)
        t_arrived(3)
        t_arrived(4)

    def new_factor(f, q, h):
        rows, cols = slice(q * PIECE, (q + 1) * PIECE), slice(h * HALF, (h + 1) * HALF)
        return DECAY_RATE * fac[f, rows, cols] + (1.0 - DECAY_RATE) * tb[f, 2 * q + h].astype(F32)

    def eigen_start():
        for cp in factor_loads:
            cp.wait()
        pltpu.make_async_copy(basis_in, ebas, lsem.at[7]).wait()
        eigs[...] = jnp.zeros_like(eigs)

    def eigen_rows(q):
        rows = slice(q * PIECE, (q + 1) * PIECE)
        prod = jnp.zeros((PIECE, FB), F32)
        for h in range(2):
            new = DECAY_RATE * fac[c, rows, h * HALF : (h + 1) * HALF] + (1.0 - DECAY_RATE) * tb[
                c, 2 * q + h
            ].astype(F32)
            basis = ebas[h * HALF : (h + 1) * HALF, :]
            for _ in range(3):
                part = new.astype(BF)
                prod = prod + ndot(part, basis)
                new = new - part.astype(F32)
        prod = prod * ebas[rows, :].astype(F32)
        eigs[...] += jnp.sum(prod.reshape(PIECE // 8, 8, FB), axis=0)

    def factor_outputs():
        for o in range(NF):
            t_core_recv(o).wait_recv()
        for q in range(4):
            for h in range(2):
                rows, cols = slice(q * PIECE, (q + 1) * PIECE), slice(h * HALF, (h + 1) * HALF)
                act_new[rows, cols] = new_factor(0, q, h)
                grad_new[rows, cols] = new_factor(1, q, h)

    def eigen_end():
        eig = jnp.broadcast_to(jnp.sum(eigs[...], axis=0, keepdims=True), (8, FB))

        @pl.when(c == 0)
        def _():
            eigb[0] = eig
            rc(eigb.at[0], eigb.at[0], ec_ss, ec_rs, core).start()

        @pl.when((c == 1) & (w == z))
        def _():
            eigb[1] = eig
            for k in range(1, 8):
                rc(eigb.at[1], eigb.at[1], e_ss.at[k - 1], e_rs, (r, (w + k) % 8)).start()

    def eigen_pass():
        @pl.when(c == 1)
        def _():
            @pl.when(w != z)
            def _():
                rc(eigb.at[1], eigb.at[1], e_ss.at[0], e_rs, (r, z)).wait_recv()

            rc(eigb.at[1], eigb.at[1], ec_ss, ec_rs, core).start()

    lags = (0, 2, 7, 12, 17, 22)
    compute_factor()
    each_factor(merge)
    run(12, lags)
    advance(1, 12)
    each_factor(hop_1)
    wait_piece(5)
    fwd_p(0).start()
    send_p(2).start()
    wait_piece(4)
    fwd_m(0).start()
    send_m(2).start()
    run(14, lags)
    advance(1, 14)
    advance(2, 12)
    each_factor(hop_2)
    wait_piece(7)
    fwd_p(1).start()
    send_p(3).start()
    wait_piece(6)
    fwd_m(1).start()
    send_m(3).start()
    run(16, lags)
    recv_x(0).wait_recv()
    run(20, lags)
    advance(1, 20)
    advance(3, 12)
    advance(2, 14)
    spread_1()
    wait_piece(8)
    wait_piece(9)
    run(23, lags)
    advance(1, 23)
    advance(4, 12)
    advance(3, 14)
    advance(2, 20)
    spread_2()
    wait_piece(10)
    wait_piece(11)
    run(26, lags)
    recv_x(1).wait_recv()
    run(32, lags)
    spread_3()
    wait_piece(12)
    wait_piece(13)
    run(36, lags)
    wait_piece(14)
    wait_piece(15)
    run(40, lags)
    advance(1, 40)
    eigen_start()
    for to in range(41, 40 + 23):
        advance_all(to, lags)
        if to in (42, 45, 48, 51):
            eigen_rows((to - 42) // 3)
        if to == 51:
            eigen_end()
        if to == 56:
            factor_outputs()
    eigen_pass()

    pltpu.make_async_copy(basis_out.at[z], bout, lsem.at[6]).wait()
    def w_copy(q):
        return rc(wb.at[q], wb.at[q], w_ss.at[q], w_rs.at[q], core)

    home = (z % 2) == xl
    dy = (z // 2 - y + NY) % NY
    shard = jnp.where(dy == 3, 2, jnp.where(dy == 2, 3, dy))

    def mine_first(idx):
        return jnp.where(shard == 2, 1 - idx % 2, idx % 2) == c

    @pl.loop(0, 4)
    def _(idx):
        q = feature_block(shard, idx)

        @pl.when(mine_first(idx))
        def _():
            for h in range(2):
                @pl.when(jnp.logical_not(home))
                def _():
                    rc(xst.at[q, h], xr.at[xh, q, h], xs_ss.at[0, q, h], xs_rs.at[xh, q, h], far).wait_recv()

                rc(xst.at[q, h], xr.at[1 - xh, q, h], xs_ss.at[0, q, h], xs_rs.at[1 - xh, q, h], far).wait_recv()
                wb[q, :, h * HALF : (h + 1) * HALF] = (
                    xr[0, q, h].astype(F32) + xr[1, q, h].astype(F32)
                ).astype(BF)
            w_copy(q).start()

    @pl.loop(0, 4)
    def _(idx):
        q = feature_block(shard, idx)

        @pl.when(jnp.logical_not(mine_first(idx)))
        def _():
            w_copy(q).wait_recv()

        rows = pl.ds(pl.multiple_of(q * PIECE, PIECE), PIECE)
        right[rows, :] = ndot(wb[q], basis_in[...]).astype(BF)

    @pl.when(c == 0)
    def _():
        rc(eigb.at[1], eigb.at[1], ec_ss, ec_rs, core).wait_recv()

    @pl.when(c == 1)
    def _():
        rc(eigb.at[0], eigb.at[0], ec_ss, ec_rs, core).wait_recv()

    ei = eigb[0, 0:1, :]
    for a in range(4):
        rows = slice(a * PIECE, (a + 1) * PIECE)
        eo = jnp.transpose(jnp.broadcast_to(eigb[1, 0:1, rows], (PIECE, PIECE)))
        eo = jnp.concatenate([eo] * 4, axis=1)
        scaled[rows, :] = (tdot(bout[:, rows], right[...]) / (eo * ei + DAMPING)).astype(BF)
    mine = pl.ds(pl.multiple_of((xh * 2 + c) * PIECE, PIECE), PIECE)
    upper = ndot(bout[mine, :], scaled[...]).astype(BF)
    precond[...] = lax.dot_general(
        upper, basis_in[...], (((1,), (1,)), ((), ())), preferred_element_type=F32
    ).astype(BF)

    for k in range(4):
        send_p(k).wait_send()
        send_m(k).wait_send()
    for k in range(2):
        fwd_p(k).wait_send()
        fwd_m(k).wait_send()
        send_x(k).wait_send()

    @pl.loop(0, NU)
    def _(i):
        core_copy(i).wait_send()

        @pl.when(dist(i) != 0)
        def _():
            z_copy(i, zp, ra, a_rs).wait_send()

    rc(ts, tr, tx_ss.at[0], tx_rs.at[0], far).wait_send()
    for k in range(7):
        t_copy(z, k, zp).wait_send()
    for o in range(NF):
        t_core(o).wait_send()

    @pl.when(home)
    def _():
        @pl.loop(0, 4)
        def _(idx):
            q = feature_block(shard, idx)

            @pl.when(mine_first(idx))
            def _():
                for k in range(3):
                    for h in range(2):
                        rc(
                            xst.at[q, h], xr.at[xh, q, h], xs_ss.at[k, q, h], xs_rs.at[xh, q, h], far
                        ).wait_send()

    @pl.loop(0, 4)
    def _(idx):
        @pl.when(mine_first(idx))
        def _():
            w_copy(feature_block(shard, idx)).wait_send()

    rc(eigb.at[0], eigb.at[0], ec_ss, ec_rs, core).wait_send()

    @pl.when((c == 1) & (w == z))
    def _():
        for k in range(1, 8):
            rc(eigb.at[1], eigb.at[1], e_ss.at[k - 1], e_rs, (r, (w + k) % 8)).wait_send()


def per_device(acts, cotan, block_ids, basis_in, basis_out, act_factor, grad_factor):
    vm = pltpu.VMEM
    dma = pltpu.SemaphoreType.DMA
    unit = (PIECE, HALF)
    any_spec = pl.BlockSpec(memory_space=pltpu.HBM)
    precond, act_new, grad_new = pl.pallas_call(
        kernel,
        name="kfac",
        out_shape=(
            jax.ShapeDtypeStruct((PIECE, FB), BF),
            jax.ShapeDtypeStruct((FB, FB), F32),
            jax.ShapeDtypeStruct((FB, FB), F32),
        ),
        in_specs=[
            pl.BlockSpec(memory_space=pltpu.SMEM),
            any_spec,
            any_spec,
            pl.BlockSpec(memory_space=pltpu.VMEM),
            any_spec,
            any_spec,
            any_spec,
        ],
        out_specs=(pl.BlockSpec(memory_space=pltpu.VMEM),) * 3,
        scratch_shapes=[
            vm((8, 1024, HALF), BF),
            vm((2, 2, 1024, HALF), BF),
            vm((2, 2 * BLK, FB), BF),
            vm((NU,) + unit, F32),
            vm((NU,) + unit, BF),
            vm((NU,) + unit, BF),
            vm((NU,) + unit, BF),
            vm((NU,) + unit, BF),
            vm((NU,) + unit, BF),
            vm((NU,) + unit, BF),
            vm((NU,) + unit, BF),
            vm((2, 4, 2) + unit, BF),
            vm((4, 2) + unit, BF),
            vm((4, PIECE, FB), BF),
            vm(unit, BF),
            vm(unit, BF),
            vm((2, NF) + unit, BF),
            vm((2, FB, FB), F32),
            vm((FB, FB), BF),
            vm((FB, FB), BF),
            vm((2, 8, FB), F32),
            vm((8, FB), F32),
            vm((FB, FB), BF),
            vm((FB, FB), BF),
            dma((10,)),
            dma((12,)),
            dma((16,)),
            dma((2,)),
            dma((2,)),
            dma((NU,)),
            dma((NU,)),
            dma((NU,)),
            dma((NU,)),
            dma((NU,)),
            dma((NU,)),
            dma((NU,)),
            dma((3, 4, 2)),
            dma((2, 4, 2)),
            dma((4,)),
            dma((4,)),
            dma((7,)),
            dma((NF,)),
            dma((1,)),
            dma((1,)),
            dma((NF,)),
            dma((NF,)),
            dma((7,)),
            dma,
            dma,
            dma,
        ],
        compiler_params=pltpu.CompilerParams(
            collective_id=0, has_side_effects=True, vmem_limit_bytes=60 << 20
        ),
    )(
        block_ids,
        acts,
        cotan,
        basis_in.reshape(FB, FB),
        basis_out,
        act_factor.reshape(FB, FB),
        grad_factor.reshape(FB, FB),
    )
    return precond, act_new.reshape(1, FB, FB), grad_new.reshape(1, FB, FB)


def solution(mesh):
    return jax.shard_map(
        per_device,
        mesh=mesh,
        in_specs=(
            P("dp", "worker"),
            P("dp", "worker"),
            P("dp"),
            P("worker", None, None),
            P(),
            P("worker", None, None),
            P("worker", None, None),
        ),
        out_specs=(P("dp", "worker"), P("worker", None, None), P("worker", None, None)),
        check_vma=False,
    )
```

time: 118 us -> 99.9 us (0.85)
  the two profiles are of different devices: /device:TPU:57 before, /device:TPU:19 now
where the time goes in v2:
time: 99.9 us; the launch traced here: 99.4 us
  Pallas kernels  92.6 us (93%)
  local copies, waits for them, and re-layouts  6.09 us (6%)
    pallas_call x1, Pallas kernels, per_device(): pl.pallas_call(kernel, name='kfac', out_shape=(jax.ShapeDtypeStruct((PIEC...  92.6 us
    unnamed x3, local copies, waits for them, and re-layouts  6.09 us

profile of v2, /device:TPU:19, one launch (start us, length us, event | category | flops | bytes accessed | tf_op | source)
XLA Modules:
  0.0 99.4 jit_solution(17446422491840939406)
XLA Ops:
  0.6 92.6 %kfac.1 = (bf16[128,512]{1,0:T(8,128)(2,1)}, f32[512,512]{1,0:T(8,128)}, f32[512,512]{1,0:T(8,128)}) custom-call(s32[2]{0:T(128)} %ids.1, bf16[1024,512]{1,0:T(8,128)(2,1)} %acts.1, bf16[1024,512]{1,0:T(8,128)(2,1)} %cotan.1, bf16[512,512]{1,0:T(8,128)(2,1)} %bitcast.9, bf16[8,512,512]{2,1,0:T(8,128)(2,1)} %basis_out.1, f32[512,512]{1,0:T(8,128)} %bitcast.5, ...), custom_call_target="tpu_custom_call" | custom-call | tf_op jit(solution)/shard_map/kfac/pallas_call | solution.py:632
  93.3 1.6 %copy.13 = bf16[128,512]{1,0:T(8,128)(2,1)} copy(bf16[128,512]{1,0:T(8,128)(2,1)} %get-tuple-element.12) | data formatting | bytes 262144
  94.9 2.3 %copy.14 = f32[1,512,512]{2,1,0:T(8,128)} copy(f32[1,512,512]{2,1,0:T(8,128)} %bitcast.8) | data formatting | bytes 2097152
  97.1 2.3 %copy.15 = f32[1,512,512]{2,1,0:T(8,128)} copy(f32[1,512,512]{2,1,0:T(8,128)} %bitcast.7) | data formatting | bytes 2097152

commit v3 on v2

--- a/solution.py
+++ b/solution.py
@@ -15,7 +15,7 @@
 HALF = 256
 NF = 8
 NU = 40
-TREE_FROM = 40
+SKIP_FROM = 36
 BF = jnp.bfloat16
 F32 = jnp.float32
 
@@ -79,7 +79,7 @@
 
 def kernel(
     ids, acts, cotan, basis_in, basis_out, act_factor, grad_factor,
-    precond, act_new, grad_new,
+    precond, totals,
     cotb, actb, smp, own, cout, cin, zout, ra, rb, rcc, rd, xr, xst, wb, ts, tr, tb, fac, ebas, bout, eigb, eigs, scaled, right,
     lsem, y_ss, y_rs, x_ss, x_rs, c_ss, c_rs, z_ss, a_rs, b_rs, cc_rs, d_rs, xs_ss, xs_rs, w_ss, w_rs, t_ss, t_rs, tx_ss, tx_rs,
     tc_ss, tc_rs, e_ss, e_rs, ec_ss, ec_rs,
@@ -122,17 +122,12 @@
     @pl.when(c == 0)
     def _():
         pltpu.make_async_copy(basis_in, ebas, lsem.at[7]).start()
+        pltpu.make_async_copy(act_factor, fac, lsem.at[8]).start()
 
     @pl.when(c == 1)
     def _():
         pltpu.make_async_copy(basis_out.at[w], ebas, lsem.at[7]).start()
-
-    factor_loads = [
-        pltpu.make_async_copy(act_factor, fac.at[0], lsem.at[8]),
-        pltpu.make_async_copy(grad_factor, fac.at[1], lsem.at[9]),
-    ]
-    for cp in factor_loads:
-        cp.start()
+        pltpu.make_async_copy(grad_factor, fac, lsem.at[8]).start()
 
     barrier = pltpu.get_barrier_semaphore()
     for k in range(1, 8):
@@ -184,6 +179,9 @@
         to = jnp.where(i < NF, i, 2 * ((y + y_offset(k)) % NY) + xl)
         return (to - z + NZ) % NZ
 
+    def along(i, steps):
+        return at(dz=jnp.where(i % 2 == 0, steps, NZ - steps))
+
     def core_copy(i):
         return rc(cout.at[i], cin.at[i], c_ss.at[i], c_rs.at[i], core)
 
@@ -192,8 +190,8 @@
 
     lands = {"a": (ra, a_rs), "b": (rb, b_rs), "c": (rcc, cc_rs), "d": (rd, d_rs)}
 
-    def send_z(i, dev, slot):
-        z_copy(i, dev, *lands[slot]).start()
+    def send_z(i, steps, slot):
+        z_copy(i, along(i, steps), *lands[slot]).start()
 
     def recv_z(i, slots):
         for slot in slots:
@@ -237,45 +235,47 @@
         core_copy(i).start()
         own[i] = jnp.where(lower, both[:PIECE], both[PIECE:])
 
-    def is_tree(i):
-        return (i >= TREE_FROM) | (i < NF)
+    def way(i):
+        d = dist(i)
+        return jnp.where(i % 2 == 0, d, (NZ - d) % NZ), i < NF, (i >= NF) & (i < SKIP_FROM), i >= SKIP_FROM
 
     def merge(i):
         core_copy(i).wait_recv()
         acc = own[i] + cin[i].astype(F32)
         own[i] = acc
-        d = dist(i)
-        tree = is_tree(i)
-        far_up = d == 4
-        far_down = d == 5
-        near_up = tree & ((d == 1) | (d == 3))
+        d, tree, chain, skip = way(i)
+        near_up = (tree & ((d == 1) | (d == 3))) | (skip & (d == 3))
         near_down = tree & (d == 7)
 
-        @pl.when(far_up | far_down | near_up | near_down)
+        @pl.when((d == 4) | (d == 5) | near_up | near_down)
         def _():
             zout[i] = acc.astype(BF)
 
-        @pl.when(far_up & tree)
-        def _():
-            send_z(i, zp2, "a")
-
-        @pl.when((far_up & jnp.logical_not(tree)) | (near_up & (d == 1)))
-        def _():
-            send_z(i, zp, "a")
-
-        @pl.when(near_up & (d == 3))
-        def _():
-            send_z(i, zp, "b")
-
-        @pl.when(far_down | near_down)
-        def _():
-            send_z(i, zm, "b")
-
-    def pass_on(i, cond, slots, dev, slot):
+        @pl.when((d == 4) & tree)
+        def _():
+            send_z(i, 2, "a")
+
+        @pl.when((d == 4) & skip)
+        def _():
+            send_z(i, 2, "c")
+
+        @pl.when(((d == 4) & chain) | (tree & (d == 1)) | (skip & (d == 3)))
+        def _():
+            send_z(i, 1, "a")
+
+        @pl.when(tree & (d == 3))
+        def _():
+            send_z(i, 1, "b")
+
+        @pl.when((d == 5) | near_down)
+        def _():
+            send_z(i, 7, "b")
+
+    def pass_on(i, cond, slots, steps, slot):
         @pl.when(cond)
         def _():
             zout[i] = recv_z(i, slots)
-            send_z(i, dev, slot)
+            send_z(i, steps, slot)
 
     def finish_z(i, cond, slots):
         @pl.when(cond)
@@ -304,25 +304,27 @@
                     rc(xst.at[q, h], xr.at[xh, q, h], xs_ss.at[2, q, h], xs_rs.at[xh, q, h], cross).start()
 
     def hop_1(i):
-        d, tree = dist(i), is_tree(i)
-        chain = jnp.logical_not(tree)
-        pass_on(i, (d == 3) & chain, "a", zp, "a")
-        pass_on(i, (d == 6) & chain, "b", zm, "b")
-        pass_on(i, (d == 2) & tree, "ab", zp2, "c")
-        pass_on(i, (d == 6) & tree, "b", zm2, "d")
+        d, tree, chain, skip = way(i)
+        pass_on(i, (d == 3) & chain, "a", 1, "a")
+        pass_on(i, (d == 2) & skip, "ac", 1, "a")
+        pass_on(i, (d == 6) & (chain | skip), "b", 7, "b")
+        pass_on(i, (d == 2) & tree, "ab", 2, "c")
+        pass_on(i, (d == 6) & tree, "b", 6, "d")
 
     def hop_2(i):
-        d, tree = dist(i), is_tree(i)
-        chain = jnp.logical_not(tree)
-        pass_on(i, (d == 2) & chain, "a", zp, "a")
-        pass_on(i, (d == 7) & chain, "b", zm, "b")
+        d, tree, chain, skip = way(i)
+        pass_on(i, ((d == 2) & chain) | ((d == 1) & skip), "a", 1, "a")
+        pass_on(i, (d == 7) & (chain | skip), "b", 7, "b")
         finish_z(i, (d == 0) & tree, "abcd")
 
     def hop_3(i):
-        pass_on(i, (dist(i) == 1) & jnp.logical_not(is_tree(i)), "a", zp, "a")
+        d, _, chain, skip = way(i)
+        pass_on(i, (d == 1) & chain, "a", 1, "a")
+        finish_z(i, (d == 0) & skip, "ab")
 
     def hop_4(i):
-        finish_z(i, (dist(i) == 0) & jnp.logical_not(is_tree(i)), "ab")
+        d, _, chain, _ = way(i)
+        finish_z(i, (d == 0) & chain, "ab")
 
     stages = (compute, merge, hop_1, hop_2, hop_3, hop_4)
     done = [NF] * len(stages)
@@ -384,11 +386,12 @@
         t_core(o).start()
 
     def spread_2():
-        t_arrived(6)
-        t_copy(origin(6), 4, zp).start()
-        t_copy(origin(6), 5, zp2).start()
-        t_arrived(2)
-        t_copy(origin(2), 6, zm).start()
+        back, ahead = jnp.where(c == 0, 6, 2), jnp.where(c == 0, 2, 6)
+        t_arrived(back)
+        t_copy(origin(back), 4, along(c, 1)).start()
+        t_copy(origin(back), 5, along(c, 2)).start()
+        t_arrived(ahead)
+        t_copy(origin(ahead), 6, along(c, 7)).start()
         t_arrived(7)
         t_arrived(1)
 
@@ -397,39 +400,37 @@
         t_arrived(3)
         t_arrived(4)
 
-    def new_factor(f, q, h):
-        rows, cols = slice(q * PIECE, (q + 1) * PIECE), slice(h * HALF, (h + 1) * HALF)
-        return DECAY_RATE * fac[f, rows, cols] + (1.0 - DECAY_RATE) * tb[f, 2 * q + h].astype(F32)
-
-    def eigen_start():
-        for cp in factor_loads:
-            cp.wait()
-        pltpu.make_async_copy(basis_in, ebas, lsem.at[7]).wait()
-        eigs[...] = jnp.zeros_like(eigs)
-
-    def eigen_rows(q):
-        rows = slice(q * PIECE, (q + 1) * PIECE)
-        prod = jnp.zeros((PIECE, FB), F32)
-        for h in range(2):
-            new = DECAY_RATE * fac[c, rows, h * HALF : (h + 1) * HALF] + (1.0 - DECAY_RATE) * tb[
-                c, 2 * q + h
-            ].astype(F32)
-            basis = ebas[h * HALF : (h + 1) * HALF, :]
+    def eigen_chunks(lo, hi):
+        if lo == 6:
+            pltpu.make_async_copy(act_factor, fac, lsem.at[8]).wait()
+            pltpu.make_async_copy(basis_in, ebas, lsem.at[7]).wait()
+            eigs[...] = jnp.zeros_like(eigs)
+
+        @pl.loop(lo, hi)
+        def _(dz):
+            o = (z + dz) % NZ
+            rows = pl.ds(pl.multiple_of((o // 2) * PIECE, PIECE), PIECE)
+            cols = pl.ds(pl.multiple_of((o % 2) * HALF, HALF), HALF)
+            new = DECAY_RATE * fac[rows, cols] + (1.0 - DECAY_RATE) * tb[c, o].astype(F32)
+            basis = ebas[cols, :]
+            prod = jnp.zeros((PIECE, FB), F32)
             for _ in range(3):
                 part = new.astype(BF)
                 prod = prod + ndot(part, basis)
                 new = new - part.astype(F32)
-        prod = prod * ebas[rows, :].astype(F32)
-        eigs[...] += jnp.sum(prod.reshape(PIECE // 8, 8, FB), axis=0)
+            prod = prod * ebas[rows, :].astype(F32)
+            eigs[...] += jnp.sum(prod.reshape(PIECE // 8, 8, FB), axis=0)
+
+    def total_copy(f, o):
+        into = totals.at[f, pl.ds((o // 2) * PIECE, PIECE), pl.ds((o % 2) * HALF, HALF)]
+        return pltpu.make_async_copy(tb.at[f, o], into, lsem.at[10 + f * NF + o])
 
     def factor_outputs():
         for o in range(NF):
             t_core_recv(o).wait_recv()
-        for q in range(4):
-            for h in range(2):
-                rows, cols = slice(q * PIECE, (q + 1) * PIECE), slice(h * HALF, (h + 1) * HALF)
-                act_new[rows, cols] = new_factor(0, q, h)
-                grad_new[rows, cols] = new_factor(1, q, h)
+        for f in range(2):
+            for o in range(NF):
+                total_copy(f, o).start()
 
     def eigen_end():
         eig = jnp.broadcast_to(jnp.sum(eigs[...], axis=0, keepdims=True), (8, FB))
@@ -491,6 +492,7 @@
     advance(3, 14)
     advance(2, 20)
     spread_2()
+    eigen_chunks(6, 11)
     wait_piece(10)
     wait_piece(11)
     run(26, lags)
@@ -504,15 +506,13 @@
     wait_piece(15)
     run(40, lags)
     advance(1, 40)
-    eigen_start()
-    for to in range(41, 40 + 23):
+    eigen_chunks(3, 6)
+    eigen_end()
+    for to in range(41, 53):
         advance_all(to, lags)
-        if to in (42, 45, 48, 51):
-            eigen_rows((to - 42) // 3)
-        if to == 51:
-            eigen_end()
-        if to == 56:
-            factor_outputs()
+    factor_outputs()
+    for to in range(53, 40 + 23):
+        advance_all(to, lags)
     eigen_pass()
 
     pltpu.make_async_copy(basis_out.at[z], bout, lsem.at[6]).wait()
@@ -623,19 +623,28 @@
         for k in range(1, 8):
             rc(eigb.at[1], eigb.at[1], e_ss.at[k - 1], e_rs, (r, (w + k) % 8)).wait_send()
 
+    for f in range(2):
+        for o in range(NF):
+            total_copy(f, o).wait()
+
+
+def update(precond, totals, act_factor, grad_factor, precond_out, act_new, grad_new):
+    precond_out[...] = precond[...]
+    act_new[0] = DECAY_RATE * act_factor[0] + (1.0 - DECAY_RATE) * totals[0].astype(F32)
+    grad_new[0] = DECAY_RATE * grad_factor[0] + (1.0 - DECAY_RATE) * totals[1].astype(F32)
+
 
 def per_device(acts, cotan, block_ids, basis_in, basis_out, act_factor, grad_factor):
     vm = pltpu.VMEM
     dma = pltpu.SemaphoreType.DMA
     unit = (PIECE, HALF)
     any_spec = pl.BlockSpec(memory_space=pltpu.HBM)
-    precond, act_new, grad_new = pl.pallas_call(
+    precond, totals = pl.pallas_call(
         kernel,
         name="kfac",
         out_shape=(
             jax.ShapeDtypeStruct((PIECE, FB), BF),
-            jax.ShapeDtypeStruct((FB, FB), F32),
-            jax.ShapeDtypeStruct((FB, FB), F32),
+            jax.ShapeDtypeStruct((2, FB, FB), BF),
         ),
         in_specs=[
             pl.BlockSpec(memory_space=pltpu.SMEM),
@@ -646,7 +655,7 @@
             any_spec,
             any_spec,
         ],
-        out_specs=(pl.BlockSpec(memory_space=pltpu.VMEM),) * 3,
+        out_specs=(pl.BlockSpec(memory_space=pltpu.VMEM),) * 2,
         scratch_shapes=[
             vm((8, 1024, HALF), BF),
             vm((2, 2, 1024, HALF), BF),
@@ -665,14 +674,14 @@
             vm(unit, BF),
             vm(unit, BF),
             vm((2, NF) + unit, BF),
-            vm((2, FB, FB), F32),
+            vm((FB, FB), F32),
             vm((FB, FB), BF),
             vm((FB, FB), BF),
             vm((2, 8, FB), F32),
             vm((8, FB), F32),
             vm((FB, FB), BF),
             vm((FB, FB), BF),
-            dma((10,)),
+            dma((26,)),
             dma((12,)),
             dma((16,)),
             dma((2,)),
@@ -711,7 +720,23 @@
         act_factor.reshape(FB, FB),
         grad_factor.reshape(FB, FB),
     )
-    return precond, act_new.reshape(1, FB, FB), grad_new.reshape(1, FB, FB)
+    steps = 4
+    rows = pl.BlockSpec((PIECE // steps, FB), lambda i: (i, 0))
+    both = pl.BlockSpec((2, FB // steps, FB), lambda i: (0, i, 0))
+    factor = pl.BlockSpec((1, FB // steps, FB), lambda i: (0, i, 0))
+    return pl.pallas_call(
+        update,
+        name="update",
+        grid=(steps,),
+        in_specs=[rows, both, factor, factor],
+        out_specs=(rows, factor, factor),
+        out_shape=(
+            jax.ShapeDtypeStruct((PIECE, FB), BF),
+            jax.ShapeDtypeStruct((1, FB, FB), F32),
+            jax.ShapeDtypeStruct((1, FB, FB), F32),
+        ),
+        compiler_params=pltpu.CompilerParams(vmem_limit_bytes=60 << 20),
+    )(precond, totals, act_factor, grad_factor)
 
 
 def solution(mesh):

time: 99.9 us -> 92.5 us (0.926)
  local copies, waits for them, and re-layouts: 6.09 us -> 0 us
    unnamed x3 -> x0, local copies, waits for them, and re-layouts: 6.09 us -> none
    pallas_call x1, Pallas kernels: 92.6 us -> 87.7 us  [per_device(): pl.pallas_call(kernel, name='kfac', out_shape=(jax.ShapeDtypeStruct((PIEC...]
    pallas_call x0 -> x1, Pallas kernels: none -> 4 us  [per_device(): pl.pallas_call(update, name='update', grid=(steps,), in_specs=[rows, both...]
where the time goes in v3:
time: 92.5 us; the launch traced here: 92.3 us
  Pallas kernels  91.7 us (99%)
    pallas_call x1, Pallas kernels, per_device(): pl.pallas_call(kernel, name='kfac', out_shape=(jax.ShapeDtypeStruct((PIEC...  87.7 us
    pallas_call x1, Pallas kernels, per_device(): pl.pallas_call(update, name='update', grid=(steps,), in_specs=[rows, both...  4 us

profile of v3, /device:TPU:19, one launch (start us, length us, event | category | flops | bytes accessed | tf_op | source)
XLA Modules:
  0.0 92.3 jit_solution(12533744531725882382)
XLA Ops:
  0.6 87.7 %kfac.1 = (bf16[128,512]{1,0:T(8,128)(2,1)}, bf16[2,512,512]{2,1,0:T(8,128)(2,1)}) custom-call(s32[2]{0:T(128)} %ids.1, bf16[1024,512]{1,0:T(8,128)(2,1)} %acts.1, bf16[1024,512]{1,0:T(8,128)(2,1)} %cotan.1, bf16[512,512]{1,0:T(8,128)(2,1)} %bitcast.5, bf16[8,512,512]{2,1,0:T(8,128)(2,1)} %basis_out.1, f32[512,512]{1,0:T(8,128)} %bitcast.3, f32[512,512]{1,0:T(8,128)} %bitcast.4), custom_call_target="tpu_custom_call" | custom-call | tf_op jit(solution)/shard_map/kfac/pallas_call | solution.py:642
  88.3 4.0 %update.1 = (bf16[128,512]{1,0:T(8,128)(2,1)}, f32[1,512,512]{2,1,0:T(8,128)}, f32[1,512,512]{2,1,0:T(8,128)}) custom-call(bf16[128,512]{1,0:T(8,128)(2,1)} %get-tuple-element.5.precond, bf16[2,512,512]{2,1,0:T(8,128)(2,1)} %get-tuple-element.6.totals, f32[1,512,512]{2,1,0:T(8,128)} %act_factor.1, f32[1,512,512]{2,1,0:T(8,128)} %grad_factor.1), custom_call_target="tpu_custom_call" | custom-call | tf_op jit(solution)/shard_map/update/pallas_call | solution.py:727

commit v4 on v3

--- a/solution.py
+++ b/solution.py
@@ -32,28 +32,46 @@
     return (z * 4 + (x // 2) * 2 + c, y * 2 + x % 2)
 
 
+def weight_units():
+    units = [(m, 0, h) for m in range(4) for h in range(2)]
+    units += [(m, 1, 0) for m in range(4)]
+    for m in (4, 5):
+        units += [(m, 0, 0), (m, 0, 1), (m, 1, 0)]
+    units += [(m, 1, 1) for m in range(6)]
+    return units + [(m, e, h) for m in (6, 7) for e in range(2) for h in range(2)]
+
+
+def packed(values, bits):
+    word = sum(v << (bits * k) for k, v in enumerate(values))
+    return word - (1 << 32) if word >= 1 << 31 else word
+
+
+def field(word, place, bits):
+    return lax.shift_right_logical(word, jnp.int32(bits) * place) & ((1 << bits) - 1)
+
+
+PAIR_ACTS = [packed([2 * m + e for m, e, _ in weight_units()[g : g + 8]], 4) for g in range(0, 32, 8)]
+PART = packed([h for _, _, h in weight_units()], 1)
+
+
+def shard_offset(m, c):
+    side = 1 - c if m in (3, 7) else c
+    return 0 if m < 2 else 2 if m in (4, 6) else 3 if side else 1
+
+
+OFFSETS = [
+    [packed([shard_offset(m, c) for m, _, _ in weight_units()[g : g + 16]], 2) for g in (0, 16)] for c in range(2)
+]
+
+
 def unit_parts(i):
     j = i - NF
-    runs = (
-        (0, 0, 0, None),
-        (8, 0, 1, 0),
-        (12, 4, 0, None),
-        (14, 4, 1, 0),
-        (15, 5, 0, None),
-        (17, 5, 1, 0),
-        (18, 0, 1, 1),
-    )
-    m, e, h = j, j, j
-    for lo, pair, acts, half in runs:
-        here = j >= lo
-        m = jnp.where(here, pair + ((j - lo) // 2 if half is None else j - lo), m)
-        e = jnp.where(here, acts, e)
-        h = jnp.where(here, (j - lo) % 2 if half is None else half, h)
-    late = j >= 24
-    m = jnp.where(late, 6 + (j - 24) // 4, m)
-    e = jnp.where(late, (j // 2) % 2, e)
-    h = jnp.where(late, j % 2, h)
-    return m, e, h
+    group = j >> 3
+    word = jnp.int32(PAIR_ACTS[0])
+    for g in range(1, 4):
+        word = jnp.where(group == g, jnp.int32(PAIR_ACTS[g]), word)
+    both = field(word, j & 7, 4)
+    return both >> 1, both & 1, field(jnp.int32(PART), j, 1)
 
 
 def kept_piece(m, c):
@@ -174,10 +192,13 @@
     for cp in loads[:6]:
         cp.wait()
 
+    offsets = [jnp.where(c == 0, jnp.int32(OFFSETS[0][g]), jnp.int32(OFFSETS[1][g])) for g in range(2)]
+
     def dist(i):
-        k, _ = piece_source(kept_piece(unit_parts(i)[0], c))
-        to = jnp.where(i < NF, i, 2 * ((y + y_offset(k)) % NY) + xl)
-        return (to - z + NZ) % NZ
+        j = i - NF
+        dy = field(jnp.where(j < 16, offsets[0], offsets[1]), j & 15, 2)
+        to = jnp.where(i < NF, i, 2 * ((y + dy) & (NY - 1)) + xl)
+        return (to - z + NZ) & (NZ - 1)
 
     def along(i, steps):
         return at(dz=jnp.where(i % 2 == 0, steps, NZ - steps))
@@ -720,7 +741,7 @@
         act_factor.reshape(FB, FB),
         grad_factor.reshape(FB, FB),
     )
-    steps = 4
+    steps = 2
     rows = pl.BlockSpec((PIECE // steps, FB), lambda i: (i, 0))
     both = pl.BlockSpec((2, FB // steps, FB), lambda i: (0, i, 0))
     factor = pl.BlockSpec((1, FB // steps, FB), lambda i: (0, i, 0))

time: 92.5 us -> 89 us (0.962)
  Pallas kernels: 91.7 us -> 88.2 us
    pallas_call x1, Pallas kernels: 87.7 us -> 85.2 us  [per_device(): pl.pallas_call(kernel, name='kfac', out_shape=(jax.ShapeDtypeStruct((PIEC...]
    pallas_call x1, Pallas kernels: 4 us -> 2.97 us  [per_device(): pl.pallas_call(update, name='update', grid=(steps,), in_specs=[rows, both...]
where the time goes in v4:
time: 89 us; the launch traced here: 88.8 us
  Pallas kernels  88.2 us (99%)
    pallas_call x1, Pallas kernels, per_device(): pl.pallas_call(kernel, name='kfac', out_shape=(jax.ShapeDtypeStruct((PIEC...  85.2 us
    pallas_call x1, Pallas kernels, per_device(): pl.pallas_call(update, name='update', grid=(steps,), in_specs=[rows, both...  2.97 us

profile of v4, /device:TPU:19, one launch (start us, length us, event | category | flops | bytes accessed | tf_op | source)
XLA Modules:
  0.0 88.8 jit_solution(2436678798952733577)
XLA Ops:
  0.6 85.2 %kfac.1 = (bf16[128,512]{1,0:T(8,128)(2,1)}, bf16[2,512,512]{2,1,0:T(8,128)(2,1)}) custom-call(s32[2]{0:T(128)} %ids.1, bf16[1024,512]{1,0:T(8,128)(2,1)} %acts.1, bf16[1024,512]{1,0:T(8,128)(2,1)} %cotan.1, bf16[512,512]{1,0:T(8,128)(2,1)} %bitcast.5, bf16[8,512,512]{2,1,0:T(8,128)(2,1)} %basis_out.1, f32[512,512]{1,0:T(8,128)} %bitcast.3, f32[512,512]{1,0:T(8,128)} %bitcast.4), custom_call_target="tpu_custom_call" | custom-call | tf_op jit(solution)/shard_map/kfac/pallas_call | solution.py:663
  85.9 3.0 %update.1 = (bf16[128,512]{1,0:T(8,128)(2,1)}, f32[1,512,512]{2,1,0:T(8,128)}, f32[1,512,512]{2,1,0:T(8,128)}) custom-call(bf16[128,512]{1,0:T(8,128)(2,1)} %get-tuple-element.5.precond, bf16[2,512,512]{2,1,0:T(8,128)(2,1)} %get-tuple-element.6.totals, f32[1,512,512]{2,1,0:T(8,128)} %act_factor.1, f32[1,512,512]{2,1,0:T(8,128)} %grad_factor.1), custom_call_target="tpu_custom_call" | custom-call | tf_op jit(solution)/shard_map/update/pallas_call | solution.py:748

commit v5 on v4

--- a/solution.py
+++ b/solution.py
@@ -536,6 +536,28 @@
         advance_all(to, lags)
     eigen_pass()
 
+    for k in range(4):
+        send_p(k).wait_send()
+        send_m(k).wait_send()
+    for k in range(2):
+        fwd_p(k).wait_send()
+        fwd_m(k).wait_send()
+        send_x(k).wait_send()
+
+    @pl.loop(0, NU)
+    def _(i):
+        core_copy(i).wait_send()
+
+        @pl.when(dist(i) != 0)
+        def _():
+            z_copy(i, zp, ra, a_rs).wait_send()
+
+    rc(ts, tr, tx_ss.at[0], tx_rs.at[0], far).wait_send()
+    for k in range(7):
+        t_copy(z, k, zp).wait_send()
+    for o in range(NF):
+        t_core(o).wait_send()
+
     pltpu.make_async_copy(basis_out.at[z], bout, lsem.at[6]).wait()
     def w_copy(q):
         return rc(wb.at[q], wb.at[q], w_ss.at[q], w_rs.at[q], core)
@@ -594,28 +616,6 @@
     precond[...] = lax.dot_general(
         upper, basis_in[...], (((1,), (1,)), ((), ())), preferred_element_type=F32
     ).astype(BF)
-
-    for k in range(4):
-        send_p(k).wait_send()
-        send_m(k).wait_send()
-    for k in range(2):
-        fwd_p(k).wait_send()
-        fwd_m(k).wait_send()
-        send_x(k).wait_send()
-
-    @pl.loop(0, NU)
-    def _(i):
-        core_copy(i).wait_send()
-
-        @pl.when(dist(i) != 0)
-        def _():
-            z_copy(i, zp, ra, a_rs).wait_send()
-
-    rc(ts, tr, tx_ss.at[0], tx_rs.at[0], far).wait_send()
-    for k in range(7):
-        t_copy(z, k, zp).wait_send()
-    for o in range(NF):
-        t_core(o).wait_send()
 
     @pl.when(home)
     def _():

time: 89 us -> 88.3 us (level)
  no operation moved by 1% of the time
where the time goes in v5:
time: 88.3 us; the launch traced here: 88.1 us
  Pallas kernels  87.5 us (99%)
    pallas_call x1, Pallas kernels, per_device(): pl.pallas_call(kernel, name='kfac', out_shape=(jax.ShapeDtypeStruct((PIEC...  84.5 us
    pallas_call x1, Pallas kernels, per_device(): pl.pallas_call(update, name='update', grid=(steps,), in_specs=[rows, both...  2.97 us

profile of v5, /device:TPU:19, one launch (start us, length us, event | category | flops | bytes accessed | tf_op | source)
XLA Modules:
  0.0 88.1 jit_solution(17397718885101412424)
XLA Ops:
  0.6 84.5 %kfac.1 = (bf16[128,512]{1,0:T(8,128)(2,1)}, bf16[2,512,512]{2,1,0:T(8,128)(2,1)}) custom-call(s32[2]{0:T(128)} %ids.1, bf16[1024,512]{1,0:T(8,128)(2,1)} %acts.1, bf16[1024,512]{1,0:T(8,128)(2,1)} %cotan.1, bf16[512,512]{1,0:T(8,128)(2,1)} %bitcast.5, bf16[8,512,512]{2,1,0:T(8,128)(2,1)} %basis_out.1, f32[512,512]{1,0:T(8,128)} %bitcast.3, f32[512,512]{1,0:T(8,128)} %bitcast.4), custom_call_target="tpu_custom_call" | custom-call | tf_op jit(solution)/shard_map/kfac/pallas_call | solution.py:663
  85.2 3.0 %update.1 = (bf16[128,512]{1,0:T(8,128)(2,1)}, f32[1,512,512]{2,1,0:T(8,128)}, f32[1,512,512]{2,1,0:T(8,128)}) custom-call(bf16[128,512]{1,0:T(8,128)(2,1)} %get-tuple-element.5.precond, bf16[2,512,512]{2,1,0:T(8,128)(2,1)} %get-tuple-element.6.totals, f32[1,512,512]{2,1,0:T(8,128)} %act_factor.1, f32[1,512,512]{2,1,0:T(8,128)} %grad_factor.1), custom_call_target="tpu_custom_call" | custom-call | tf_op jit(solution)/shard_map/update/pallas_call | solution.py:748
